TPU v7x, 128 devices: a whole 4x4x4 slice. The times are simulated.
128 devices in a mesh: owner: 32 (over x, z, core), loop: 4 (over y).
Axes of the slice: x: 4, y: 4, z: 4, core: 2. Of those that a mesh axis runs over, the one named last changes fastest.
Arguments:
- embeddings: bfloat16 [131072, 768], P(('owner', 'loop'))
- cluster_ids: int32 [131072], P(('owner', 'loop')), may hold values from 0 to 31, as said below
- row_order: int32 [131072], P(('owner', 'loop')), may hold values from 0 to 131071, each once
Outputs:
- best_similarity: float32 [131072], P(('owner', 'loop'))
Inputs may be any that keep to these rules, and one draw needn't show every extreme that they name: `cluster_ids`: cluster c belongs to owner c. No device holds more than 64 rows of any one cluster, and one cluster, the same for every device, gets exactly 64 rows from each device.
All inputs are finite; a program needn't handle non-finite values.
Results may differ from a plain program's by a relative error of at most 0.00056.
Values may be sent and summed in bfloat16 or wider, within the bound.
A program may use at most 64 MiB of HBM per device.

v0:
```python
import math

import jax
import jax.numpy as jnp
from jax import lax
from jax.sharding import PartitionSpec as P

epsilon = 1e-06


def normalize_rows(values):
    wide = values.astype(jnp.float32)
    scale = lax.rsqrt(jnp.sum(wide * wide, axis=-1, keepdims=True) + epsilon)
    return (wide * scale).astype(jnp.bfloat16)


def tile_maxima(queries, query_cluster, query_order, keys, key_cluster, key_order):
    count = queries.shape[0]
    block = math.gcd(512, count)
    query_blocks = queries.reshape(count // block, block, queries.shape[1])
    cluster_blocks = query_cluster.reshape(count // block, block)
    order_blocks = query_order.reshape(count // block, block)

    def one_block(items):
        block_rows, block_cluster, block_order = items
        scores = jnp.einsum("qd,kd->qk", block_rows, keys, preferred_element_type=jnp.float32)
        same = block_cluster[:, None] == key_cluster[None, :]
        row_mask = same & (key_order[None, :] < block_order[:, None])
        row_best = jnp.max(jnp.where(row_mask, scores, -1.0), axis=1)
        return row_best

    found = lax.map(one_block, (query_blocks, cluster_blocks, order_blocks))
    return found.reshape(count)


def on_device(embeddings, cluster_ids, row_order):
    rows = embeddings.shape[0]
    owners = lax.axis_size("owner")
    capacity = 2 * rows // owners
    slots = owners * capacity
    hits = (cluster_ids[:, None] == jnp.arange(owners, dtype=jnp.int32)[None, :]).astype(jnp.int32)
    before = jnp.cumsum(hits, axis=0) - hits
    position = cluster_ids * capacity + jnp.sum(before * hits, axis=1)
    payload = normalize_rows(embeddings)
    outgoing = jnp.zeros((slots, payload.shape[1]), jnp.bfloat16).at[position].set(payload)
    out_cluster = jnp.full((slots,), -1, jnp.int32).at[position].set(cluster_ids)
    out_order = jnp.zeros((slots,), jnp.int32).at[position].set(row_order)
    arrived, arrived_cluster, arrived_order = (
        lax.all_to_all(
            outgoing.reshape(owners, capacity, payload.shape[1]),
            "owner",
            split_axis=0,
            concat_axis=0,
            tiled=True,
        ),
        lax.all_to_all(
            out_cluster.reshape(owners, capacity), "owner", split_axis=0, concat_axis=0, tiled=True
        ),
        lax.all_to_all(
            out_order.reshape(owners, capacity), "owner", split_axis=0, concat_axis=0, tiled=True
        ),
    )
    queries = arrived.reshape(slots, payload.shape[1])
    query_cluster = arrived_cluster.reshape(slots)
    query_order = arrived_order.reshape(slots)
    keys = lax.all_gather(queries, "loop", axis=0, tiled=True)
    key_cluster = lax.all_gather(query_cluster, "loop", axis=0, tiled=True)
    key_order = lax.all_gather(query_order, "loop", axis=0, tiled=True)
    found = tile_maxima(queries, query_cluster, query_order, keys, key_cluster, key_order)
    best = jnp.maximum(jnp.full((slots,), -1.0, jnp.float32), found)
    back = lax.all_to_all(
        best.reshape(owners, capacity), "owner", split_axis=0, concat_axis=0, tiled=True
    )
    return back.reshape(slots)[position]


def solution(mesh):
    return jax.shard_map(
        on_device,
        mesh=mesh,
        in_specs=(P(("owner", "loop"), None), P(("owner", "loop")), P(("owner", "loop"))),
        out_specs=P(("owner", "loop")),
        check_vma=False,
    )
```

profile of v0, /device:TPU:1, one launch (start us, length us, event | category | flops | bytes accessed | tf_op | source)
XLA Modules:
  0.0 276.8 jit_solution(6398258020742198662)
XLA Ops:
  6.5 0.7 fusion.12
  7.2 9.0 %reduce-window.6 = s32[32,8,128]{2,1,0:T(8,128)S(1)} reduce-window(s32[32,8,128]{2,1,0:T(8,128)S(1)} %fusion.12, s32[]{:T(128)} %constant.18.clone.1), window={size=1x1x128 pad=0_0x0_0x127_0}, to_apply=%region_0.0 | reduce-window | flops 4161536 | bytes 262148 | tf_op jit(solution)/shard_map/reduce-window
  16.4 0.1 copy.6
  16.6 0.1 broadcast_add_fusion
  16.7 0.7 fusion.11
  17.4 0.7 broadcast_clamp_fusion
  18.1 1.8 fusion.3
  19.9 7.2 %scatter_custom_fusion.2 = bf16[2048,768]{1,0:T(8,128)(2,1)S(1)} fusion(s32[1024]{0:T(1024)S(1)} %get-tuple-element.65, bf16[1024,768]{1,0:T(8,128)(2,1)} %param.5, f32[1024]{0:T(1024)S(1)} %add_rsqrt_fusion, bf16[]{:T(256)} %constant.20.clone.1), kind=kCustom, calls=%fused_computation.14 | custom fusion | flops 2359296 | bytes 4722690 | tf_op jit(solution)/shard_map/scatter | solution.py:45
  27.1 48.7 %all_to_all.29 = bf16[32,64,768]{2,1,0:T(8,128)(2,1)} all-to-all(bf16[32,64,768]{2,1,0:T(8,128)(2,1)S(1)} %bitcast.43), channel_id=1, replica_groups=mesh['owner'=32,'loop'=4] {'owner'}, dimensions={0} | all-to-all | bytes 6291456 | tf_op jit(solution)/shard_map/all_to_all | solution.py:49
  75.9 4.5 %scatter_custom_fusion.1 = s32[2048]{0:T(1024)S(1)} fusion(s32[1024]{0:T(1024)S(1)} %get-tuple-element.65, s32[1024]{0:T(1024)} %param.7, s32[]{:T(128)} %constant.18.clone.1), kind=kCustom, calls=%fused_computation.28 | custom fusion | bytes 8704 | tf_op jit(solution)/shard_map/scatter | solution.py:47
  80.3 0.7 all_to_all.21
  81.0 4.0 %all-to-all-start.1 = ((s32[32,1,64]{2,1,0:T(1,128)}), s32[32,1,64]{2,1,0:T(1,128)S(1)}, u32[]{:S(2)}, u32[]{:S(2)}) async-start(s32[32,1,64]{2,1,0:T(1,128)} %all_to_all.21), calls=%async_computation.1 | async-start | bytes 32768 | tf_op jit(solution)/shard_map/all_to_all | solution.py:59
  85.0 4.5 %scatter_custom_fusion = s32[2048]{0:T(1024)S(1)} fusion(s32[1024]{0:T(1024)S(1)} %get-tuple-element.65, s32[1024]{0:T(1024)} %param.6, s32[]{:T(128)} %constant.25.clone.1), kind=kCustom, calls=%fused_computation.30 | custom fusion | bytes 8704 | tf_op jit(solution)/shard_map/scatter | solution.py:46
  89.5 0.7 all_to_all.19
  90.2 1.8 all-to-all-done.1
  91.9 5.6 %all-to-all-start = ((s32[32,1,64]{2,1,0:T(1,128)}), s32[32,1,64]{2,1,0:T(1,128)S(1)}, u32[]{:S(2)}, u32[]{:S(2)}) async-start(s32[32,1,64]{2,1,0:T(1,128)} %all_to_all.19), calls=%async_computation | async-start | bytes 32768 | tf_op jit(solution)/shard_map/all_to_all | solution.py:56
  97.6 0.6 broadcast.63
  98.1 0.7 reduce.14
  98.9 5.6 %all-to-all-done = s32[32,1,64]{2,1,0:T(1,128)S(1)} async-done(((s32[32,1,64]{2,1,0:T(1,128)}), s32[32,1,64]{2,1,0:T(1,128)S(1)}, u32[]{:S(2)}, u32[]{:S(2)}) %all-to-all-start) | async-done | bytes 8224 | tf_op jit(solution)/shard_map/all_to_all | solution.py:56
  104.5 0.7 reduce.13
  105.4 10.7 %all_gather.10 = s32[8192]{0:T(1024)S(1)} all-gather(s32[2048]{0:T(1024)S(1)} %reshape.75), channel_id=1, replica_groups=mesh['owner'=32,'loop'=4] {'loop'}, dimensions={0}, use_global_device_ids=true | all-gather | bytes 40960 | tf_op jit(solution)/shard_map/all_gather | solution.py:68
  116.1 10.3 %all_gather.9 = s32[8192]{0:T(1024)S(1)} all-gather(s32[2048]{0:T(1024)S(1)} %reshape.74), channel_id=1, replica_groups=mesh['owner'=32,'loop'=4] {'loop'}, dimensions={0}, use_global_device_ids=true | all-gather | bytes 40960 | tf_op jit(solution)/shard_map/all_gather | solution.py:67
  126.4 66.5 %all-gather.2.cloned.1.call-done = bf16[8192,768]{1,0:T(8,128)(2,1)} async-done(((bf16[2048,768]{1,0:T(8,128)(2,1)}), bf16[8192,768]{1,0:T(8,128)(2,1)}) %all-gather.2.cloned.1.call-update) | async-done | bytes 12582928 | tf_op jit(solution)/shard_map/all_gather | solution.py:66
  192.9 50.8 %while.10 = (s32[]{:T(128)}, f32[4,512]{1,0:T(4,128)S(1)}, s32[4,512]{1,0:T(4,128)S(1)}, s32[8192]{0:T(1024)S(1)}, s32[8192]{0:T(1024)S(1)}, /*index=5*/s32[4,51...) while((s32[]{:T(128)}, f32[4,512]{1,0:T(4,128)S(1)}, ...), condition=%wide.region_9.10_spmd, body=%wide.region_7.9_spmd.sunk | while | flops 6463421952 | bytes 13453933 | solution.py:32
  192.9 12.6 %select_reduce_fusion.2 = f32[512]{0:T(512)S(1)} fusion(bf16[8192,768]{1,0:T(8,128)(2,1)} %get-tuple-element.148, s32[8192]{0:T(1024)S(1)} %get-tuple-element.145, s32[8192]{0:T(1024)S(1)} %get-tuple-element.144, s32[512]{0:T(512)S(1)} %bitcast.47, s32[512]{0:T(512)S(1)} %bitcast.48, bf16[4,512,768]{2,1,0:T(8,128)(2,1)} %get-tuple-element.147, ...), kind=kOutput, calls=%fused_computation.4.clone.1 | convolution fusion | flops 6463421952 | bytes 13441536 | tf_op jit(solution)/shard_map/while/body/eval_jaxpr/qd,kd->qk/dot_general | solution.py:26
  205.6 12.6 %select_reduce_fusion.2 = f32[512]{0:T(512)S(1)} fusion(bf16[8192,768]{1,0:T(8,128)(2,1)} %get-tuple-element.148, s32[8192]{0:T(1024)S(1)} %get-tuple-element.145, s32[8192]{0:T(1024)S(1)} %get-tuple-element.144, s32[512]{0:T(512)S(1)} %bitcast.47, s32[512]{0:T(512)S(1)} %bitcast.48, bf16[4,512,768]{2,1,0:T(8,128)(2,1)} %get-tuple-element.147, ...), kind=kOutput, calls=%fused_computation.4.clone.1 | convolution fusion | flops 6463421952 | bytes 13441536 | tf_op jit(solution)/shard_map/while/body/eval_jaxpr/qd,kd->qk/dot_general | solution.py:26
  218.3 12.6 %select_reduce_fusion.2 = f32[512]{0:T(512)S(1)} fusion(bf16[8192,768]{1,0:T(8,128)(2,1)} %get-tuple-element.148, s32[8192]{0:T(1024)S(1)} %get-tuple-element.145, s32[8192]{0:T(1024)S(1)} %get-tuple-element.144, s32[512]{0:T(512)S(1)} %bitcast.47, s32[512]{0:T(512)S(1)} %bitcast.48, bf16[4,512,768]{2,1,0:T(8,128)(2,1)} %get-tuple-element.147, ...), kind=kOutput, calls=%fused_computation.4.clone.1 | convolution fusion | flops 6463421952 | bytes 13441536 | tf_op jit(solution)/shard_map/while/body/eval_jaxpr/qd,kd->qk/dot_general | solution.py:26
  231.0 12.6 %select_reduce_fusion.2 = f32[512]{0:T(512)S(1)} fusion(bf16[8192,768]{1,0:T(8,128)(2,1)} %get-tuple-element.148, s32[8192]{0:T(1024)S(1)} %get-tuple-element.145, s32[8192]{0:T(1024)S(1)} %get-tuple-element.144, s32[512]{0:T(512)S(1)} %bitcast.47, s32[512]{0:T(512)S(1)} %bitcast.48, bf16[4,512,768]{2,1,0:T(8,128)(2,1)} %get-tuple-element.147, ...), kind=kOutput, calls=%fused_computation.4.clone.1 | convolution fusion | flops 6463421952 | bytes 13441536 | tf_op jit(solution)/shard_map/while/body/eval_jaxpr/qd,kd->qk/dot_general | solution.py:26
  243.8 14.4 %all_to_all.30 = f32[32,1,64]{2,1,0:T(1,128)S(1)} all-to-all(f32[32,1,64]{2,1,0:T(1,128)S(1)} %max_broadcast_in_dim.15), channel_id=1, replica_groups=mesh['owner'=32,'loop'=4] {'owner'}, dimensions={0} | all-to-all | bytes 16384 | tf_op jit(solution)/shard_map/all_to_all | solution.py:71
  258.2 0.5 broadcast.65
  258.7 0.7 reduce.15
  259.4 10.5 %gather_fusion = f32[1024]{0:T(1024)} fusion(f32[2048]{0:T(1024)S(1)} %reshape.78, s32[1024]{0:T(1024)S(1)} %get-tuple-element.64), kind=kCustom, calls=%fused_computation | custom fusion | bytes 12288 | tf_op jit(solution)/shard_map/gather | solution.py:74
  (23 shorter events, 0.9 us)
Async XLA Ops:
  6.5 186.3 %all-gather.2.cloned.1.call-start = ((), (), s32[]{:S(2)}) async-start(), calls=%async_computation.4 | async-start | bytes 15728640 | tf_op jit(solution)/shard_map/all_gather | solution.py:66
  81.0 10.9 %all-to-all-start.1 = ((s32[32,1,64]{2,1,0:T(1,128)}), s32[32,1,64]{2,1,0:T(1,128)S(1)}, u32[]{:S(2)}, u32[]{:S(2)}) async-start(s32[32,1,64]{2,1,0:T(1,128)} %all_to_all.21), calls=%async_computation.1 | async-start | bytes 32768 | tf_op jit(solution)/shard_map/all_to_all | solution.py:59
  91.9 12.6 %all-to-all-start = ((s32[32,1,64]{2,1,0:T(1,128)}), s32[32,1,64]{2,1,0:T(1,128)S(1)}, u32[]{:S(2)}, u32[]{:S(2)}) async-start(s32[32,1,64]{2,1,0:T(1,128)} %all_to_all.19), calls=%async_computation | async-start | bytes 32768 | tf_op jit(solution)/shard_map/all_to_all | solution.py:56
Sparse Core Ops, SparseCore 0:
  76.0 116.8 all-gather.1
where the time goes:
time: 277 us
  blocking collectives  84.1 us (30%)
  waiting for transfers between devices  73.9 us (27%)
  matrix products  50.4 us (18%)
  local copies, waits for them, and re-layouts  22.9 us (8%)
  other arithmetic  22.3 us (8%)
  between operations  13.5 us (5%)
  starting transfers between devices  9.56 us (3%)
    all_gather x1, waiting for transfers between devices, on_device(): keys = lax.all_gather(queries, 'loop', axis=0, tiled=True)  66.5 us
    dot_general x4, matrix products, one_block(): jnp.einsum('qd,kd->qk', block_rows, keys, preferred_element_type=jnp.floa...  50.4 us
    all_to_all x1, blocking collectives, on_device(): lax.all_to_all(outgoing.reshape(owners, capacity, payload.shape[1]), 'own...  48.7 us
    all_to_all x1, blocking collectives, on_device(): lax.all_to_all(best.reshape(owners, capacity), 'owner', split_axis=0, con...  14.4 us
    all_gather x1, blocking collectives, on_device(): key_order = lax.all_gather(query_order, 'loop', axis=0, tiled=True)  10.7 us
    gather x1, local copies, waits for them, and re-layouts, on_device(): return back.reshape(slots)[position]  10.5 us
    all_gather x1, blocking collectives, on_device(): key_cluster = lax.all_gather(query_cluster, 'loop', axis=0, tiled=True)  10.3 us
    another operation x3, other arithmetic  9.15 us
  transfers between devices with their start and end apart: 3, of which 3 were waited for; matrix products, arithmetic and copies ran while one was open for 4% of the time, Pallas kernels for 0%

commit v1 on v0

v1 whole, which is shorter than its diff:
```python
import functools

import jax
import jax.numpy as jnp
from jax import lax
from jax.experimental import pallas as pl
from jax.experimental.pallas import tpu as pltpu
from jax.sharding import PartitionSpec as P

MESH = pl.DeviceIdType.MESH
epsilon = 1e-06
D = 768
ROWS = 1024
CAP = 64
CHUNK = 256
STEPS = 8
CHUNKS = 32
FAR = float(2 ** 20)
WINDOW = 3

OFFSETS = [
    [(0, 0), (2, 2)], [(1, 0), (3, 0)], [(0, 1), (0, 3)], [(1, 1), (3, 3)],
    [(2, 1), (2, 3)], [(1, 3), (3, 1)], [(1, 2), (3, 2)], [(2, 0), (0, 2)],
]


def place(step):
    return step // 2 + 4 * (step % 2)


KEPT = ["q", "r", "p", "p", "q", "r", "p", "p"]
TO_0 = [step for step in range(STEPS) if KEPT[step] in "pq"]
TO_2 = [step for step in range(STEPS) if KEPT[step] in "pr"]
SIDE, THIRD, LATE_2, B0, LATE_0 = 8, 12, 16, 20, 28


def plan():
    tables = []
    for role in range(4):
        even = odd = 0
        side = third = low = high = late_low = late_high = 0
        steps = []
        for s in range(STEPS + 1):
            events = {}
            if s < STEPS:
                n = place(s)
                if role == 1:
                    if s % 2 == 0:
                        ranges = [(4, odd), (SIDE, high), (LATE_2, late_high)]
                    else:
                        ranges = [(0, even), (B0, low), (LATE_0, late_low)]
                    events["A"] = (n, ranges, False)
                else:
                    ranges = [(0, even), (4, odd)]
                    if role != 3:
                        ranges += [(SIDE, side), (THIRD, third)]
                    events["A"] = (n, ranges, True)
                if s % 2 == 0:
                    even += 1
                else:
                    odd += 1
            t = s - 1
            if t >= 0 and role in (0, 2):
                if t % 2 == (0 if role == 0 else 1):
                    events["B"] = (SIDE + side, [(0, even), (4, odd), (SIDE, side), (THIRD, third)], True)
                    side += 1
                if t in (TO_0 if role == 0 else TO_2):
                    events["C"] = (THIRD + third, [(0, even), (4, odd), (SIDE, side)], False)
                    third += 1
            if t >= 0 and role == 1:
                events["B"] = (SIDE + high, [(0, even), (B0, low), (LATE_0, late_low)], False)
                high += 1
                events["C"] = (B0 + low, [(4, odd), (SIDE, high), (LATE_2, late_high)], False)
                low += 1
                if s in (2, 6):
                    events["D"] = (LATE_0 + late_low, [(4, odd), (SIDE, high)], False)
                    late_low += 1
                if s in (3, 7):
                    events["D"] = (LATE_2 + late_high, [(0, even), (B0, low)], False)
                    late_high += 1
            steps.append(events)
        tables.append(steps)
    return tables


def kernel(emb, ids, order, out, unit, onehot, packed, rows, pos_rows, ord_rows, pos_col, ord_col,
           ord_out, ord_in, ord_lane, ord_sub, row_best, col_best, staged, shares, final, back,
           send_sem, recv_sem, osend_sem, orecv_sem, ysend_sem, yrecv_sem, yosend_sem, yorecv_sem,
           share_send, share_recv, back_send, back_recv):
    owner = lax.axis_index("owner")
    loop = lax.axis_index("loop")
    x, z, core = owner // 8, lax.rem(owner // 2, 4), lax.rem(owner, 2)
    role = jnp.where(core == 0, loop, lax.rem(loop + 2, 4))

    has_role = [(role == r).astype(jnp.int32) for r in range(4)]

    def device_of_role(r):
        return owner, lax.rem(r + 2 * core, 4)

    def by_role(values):
        if all(v == values[0] for v in values):
            return values[0]
        return sum(has_role[r] * values[r] for r in range(4) if values[r])

    def peers(step, sign):
        found = []
        for h, (dx, dz) in enumerate(OFFSETS[step]):
            for dc in range(2):
                slot = 4 * place(step) + 2 * h + dc
                if slot:
                    px = lax.rem(x + (dx if sign > 0 else 4 - dx), 4)
                    pz = lax.rem(z + (dz if sign > 0 else 4 - dz), 4)
                    pc = lax.rem(core + dc, 2)
                    found.append((slot, ((px * 4 + pz) * 2 + pc, loop)))
        return found

    barrier = pltpu.get_barrier_semaphore()
    for step in range(STEPS):
        for _, peer in peers(step, 1):
            pl.semaphore_signal(barrier, 1, device_id=peer, device_id_type=MESH)
    shares[...] = jnp.full(shares.shape, -1.0, jnp.float32)
    for d in (1, 2, 3):
        pl.semaphore_signal(barrier, 1, device_id=(owner, lax.rem(loop + d, 4)), device_id_type=MESH)

    cluster = ids[...]
    dx = (cluster // 8 - x + 4) % 4
    dz = (cluster // 2 % 4 - z + 4) % 4
    dc = (cluster - core + 2) % 2
    chip = dx * 4 + dz
    slot = jnp.zeros_like(cluster)
    for step in range(STEPS):
        for h, (ox, oz) in enumerate(OFFSETS[step]):
            slot = jnp.where(chip == ox * 4 + oz, 4 * place(step) + 2 * h, slot)
    slot = slot + dc
    slot_iota = lax.broadcasted_iota(jnp.int32, (32, 128), 0)
    hits = [(slot_iota == slot[j:j + 1, :]).astype(jnp.float32) for j in range(8)]
    earlier = (lax.broadcasted_iota(jnp.int32, (128, 128), 0)
               < lax.broadcasted_iota(jnp.int32, (128, 128), 1)).astype(jnp.bfloat16)
    before = jnp.zeros((32, 1), jnp.float32)
    for j in range(8):
        prefix = jnp.dot(hits[j].astype(jnp.bfloat16), earlier, preferred_element_type=jnp.float32)
        rank = jnp.sum(hits[j] * (prefix + before), axis=0, keepdims=True)
        before = before + jnp.sum(hits[j], axis=1, keepdims=True)
        pos = slot[j:j + 1, :].astype(jnp.float32) * CAP + rank
        pos_rows[j:j + 1, :] = pos
        pos_col[j * 128:(j + 1) * 128, :] = jnp.broadcast_to(pos, (128, 128)).T
        when = order[j:j + 1, :].astype(jnp.float32) - FAR
        ord_col[j * 128:(j + 1) * 128, :] = jnp.broadcast_to(when, (128, 128)).T

    def normalize(i, _):
        r = pl.ds(pl.multiple_of(i * 128, 128), 128)
        wide = emb[r, :].astype(jnp.float32)
        scale = lax.rsqrt(jnp.sum(wide * wide, axis=-1, keepdims=True) + epsilon)
        unit[r, :] = (wide * scale).astype(jnp.bfloat16)
        return 0

    lax.fori_loop(0, ROWS // 128, normalize, 0)

    def send(step, start):
        for s, peer in peers(step, 1):
            data = pltpu.make_async_remote_copy(
                src_ref=packed.at[pl.ds(s * CAP, CAP)], dst_ref=rows.at[pl.ds(s * CAP, CAP)],
                send_sem=send_sem.at[step], recv_sem=recv_sem.at[step], device_id=peer, device_id_type=MESH)
            data.start()
            when = pltpu.make_async_remote_copy(
                src_ref=ord_out.at[s // 2], dst_ref=ord_in.at[s],
                send_sem=osend_sem.at[step], recv_sem=orecv_sem.at[step], device_id=peer, device_id_type=MESH)
            when.start()

    def exchange_wait(step, sem, osem):
        skip = 1 if step == 0 else 0
        r = pl.ds(place(step) * CHUNK + skip * CAP, CHUNK - skip * CAP)
        pltpu.make_async_copy(packed.at[r], rows.at[r], sem.at[step]).wait()
        o = pl.ds(4 * place(step) + skip, 4 - skip)
        pltpu.make_async_copy(ord_in.at[o], ord_in.at[o], osem.at[step]).wait()

    lane = lax.broadcasted_iota(jnp.int32, (1024, 128), 1).astype(jnp.float32)
    for step in range(STEPS):
        first = place(step) * CHUNK
        wanted = lax.broadcasted_iota(jnp.int32, (CHUNK, 128), 0).astype(jnp.float32) + float(first)
        for j in range(8):
            onehot[:, j * 128:(j + 1) * 128] = (
                wanted == pos_rows[j:j + 1, :]).astype(jnp.float32).astype(jnp.bfloat16)
        block = jnp.dot(onehot[...], unit[...], preferred_element_type=jnp.float32).astype(jnp.bfloat16)
        packed[first:first + CHUNK, :] = block
        for pair in range(first // 128, first // 128 + 2):
            hit = pos_col[...] == lane + float(pair * 128)
            when = jnp.sum(jnp.where(hit, ord_col[...], 0.0), axis=0, keepdims=True) + FAR
            ord_out[pair] = jnp.broadcast_to(when, (8, 128))
        if step == 0:
            rows[0:CAP, :] = block[0:CAP, :]
            ord_in[0] = ord_out[0]
            pl.semaphore_wait(barrier, 34)
        if step < WINDOW:
            send(step, True)

    def clear(i, _):
        row_best[pl.ds(pl.multiple_of(i * CHUNK, CHUNK), CHUNK), :] = jnp.full((CHUNK, 128), -1.0, jnp.float32)
        col_best[pl.ds(2 * i, 2)] = jnp.full((2, 8, 128), -1.0, jnp.float32)
        return 0

    lax.fori_loop(0, CHUNKS, clear, 0)

    def spread(n):
        for h in range(2):
            when = jnp.broadcast_to(ord_lane[2 * n + h][0:1, :], (128, 128))
            at = n * CHUNK + h * 128
            ord_sub[pl.ds(at if isinstance(at, int) else pl.multiple_of(at, 128), 128), :] = when.T

    def rows_of(n):
        at = n * CHUNK
        return pl.ds(at if isinstance(at, int) else pl.multiple_of(at, CHUNK), CHUNK)

    def scores(m, n):
        return lax.dot_general(rows[rows_of(m), :], rows[rows_of(n), :], (((1,), (1,)), ((), ())),
                               preferred_element_type=jnp.float32)

    def cross(m, n):
        s = scores(m, n)
        mine = ord_sub[rows_of(m), :]
        best = row_best[rows_of(m), :]
        for h in range(2):
            part = s[:, h * 128:(h + 1) * 128]
            mask = ord_lane[2 * n + h][0:1, :] < mine
            best = jnp.maximum(best, jnp.where(mask, part, -1.0))
            other = jnp.where(mask, -1.0, part).reshape(CHUNK // 8, 8, 128)
            col_best[2 * n + h] = jnp.maximum(col_best[2 * n + h], jnp.max(other, axis=0))
        row_best[rows_of(m), :] = best

    def alone(n):
        s = scores(n, n)
        mine = ord_sub[rows_of(n), :]
        best = row_best[rows_of(n), :]
        for h in range(2):
            mask = ord_lane[2 * n + h][0:1, :] < mine
            best = jnp.maximum(best, jnp.where(mask, s[:, h * 128:(h + 1) * 128], -1.0))
        row_best[rows_of(n), :] = best

    tables = plan()

    def meet(s, name):
        events = [tables[r][s].get(name) for r in range(4)]
        n = by_role([e[0] if e else 0 for e in events])
        depth = max(len(e[1]) for e in events if e)
        starts, counts = [], []
        for k in range(depth):
            ranges = [e[1][k] if e and k < len(e[1]) else (0, 0) for e in events]
            starts.append(by_role([r[0] for r in ranges]))
            counts.append(by_role([r[1] for r in ranges]))
        total = by_role([sum(r[1] for r in e[1]) if e else 0 for e in events])

        def body(t, _):
            m = t + starts[0]
            passed = counts[0]
            for k in range(1, depth):
                m = jnp.where(t >= passed, t - passed + starts[k], m)
                passed = passed + counts[k]
            cross(m, n)
            return 0

        if any(sum(r[1] for r in e[1]) for e in events if e):
            lax.fori_loop(0, total, body, 0)
        selves = [1 if e and e[2] else 0 for e in events]
        if any(selves):
            @pl.when(by_role(selves) == 1)
            def _():
                alone(n)

    def share_rows(src, dst, to, send_index, recv_index):
        data = pltpu.make_async_remote_copy(
            src_ref=rows.at[rows_of(src)], dst_ref=rows.at[rows_of(dst)],
            send_sem=ysend_sem.at[send_index], recv_sem=yrecv_sem.at[recv_index],
            device_id=device_of_role(to), device_id_type=MESH)
        when = pltpu.make_async_remote_copy(
            src_ref=ord_lane.at[pl.ds(2 * src, 2)], dst_ref=ord_lane.at[pl.ds(2 * dst, 2)],
            send_sem=yosend_sem.at[send_index], recv_sem=yorecv_sem.at[recv_index],
            device_id=device_of_role(to), device_id_type=MESH)
        return data, when

    sends = [[], [], [], []]

    def forward(r, src, dst, to):
        @pl.when(role == r)
        def _():
            index = len(sends[r])
            for copy in share_rows(src, dst, to, index, dst - 8):
                copy.start()
            sends[r].append((src, dst, to))

    def arrive(s, name):
        events = [tables[r][s].get(name) for r in range(4)]
        for r in range(4):
            if not events[r]:
                continue

            @pl.when(role == r)
            def _():
                n = events[r][0]
                for copy in share_rows(n, n, (r + 1) % 4, 0, n - 8):
                    copy.wait_recv()
                if r in (0, 2) and name == "C" and n in (THIRD, THIRD + 3):
                    index = len(sends[r])
                    late = LATE_0 if r == 0 else LATE_2
                    late = late + (n - THIRD) // 3
                    for copy in share_rows(n, late, 1, index, late - 8):
                        copy.start()
                    sends[r].append((n, late, 1))
                spread(n)

    low_half = lax.broadcasted_iota(jnp.int32, (8, 128), 1) < CAP
    for s in range(STEPS + 1):
        if s < STEPS:
            n = place(s)
            exchange_wait(s, send_sem, osend_sem)
            if s + WINDOW < STEPS:
                send(s + WINDOW, True)
            exchange_wait(s, recv_sem, orecv_sem)
            for h in range(2):
                ord_lane[2 * n + h] = jnp.where(low_half, ord_in[4 * n + 2 * h], ord_in[4 * n + 2 * h + 1])
            forward(0, n, B0 + s, 1)
            forward(2, n, SIDE + s, 1)
            forward(1, n, SIDE + s // 2, 0 if s % 2 == 0 else 2)
            if KEPT[s] in "pq":
                forward(3, n, THIRD + TO_0.index(s), 0)
            if KEPT[s] in "pr":
                forward(3, n, THIRD + TO_2.index(s), 2)
            spread(n)
            meet(s, "A")
        for names in ("BC", "D"):
            present = [name for name in names if any(tables[r][s].get(name) for r in range(4))]
            for name in present:
                arrive(s, name)
            for name in present:
                meet(s, name)

    def line(i):
        turned = row_best[i * 128:(i + 1) * 128, :].T
        return jnp.maximum(jnp.max(turned, axis=0, keepdims=True), jnp.max(col_best[i], axis=0, keepdims=True))

    def give(r, groups):
        @pl.when(role == r)
        def _():
            copies = []
            for to, pairs in groups:
                used = {place(step): n for n, step in pairs}
                for p in range(STEPS):
                    for h in range(2):
                        i = 2 * p + h
                        value = line(2 * used[p] + h) if p in used else jnp.full((1, 128), -1.0, jnp.float32)
                        staged[to, i // 8, i % 8:i % 8 + 1, :] = value
                copies.append(pltpu.make_async_remote_copy(
                    src_ref=staged.at[to], dst_ref=shares.at[r], send_sem=share_send.at[to],
                    recv_sem=share_recv.at[r], device_id=device_of_role(to), device_id_type=MESH))
                copies[-1].start()
            for copy in copies:
                copy.wait_send()

    give(0, [(3, [(THIRD + k, t) for k, t in enumerate(TO_0)]), (1, [(SIDE + k, 2 * k) for k in range(4)])])
    give(2, [(3, [(THIRD + k, t) for k, t in enumerate(TO_2)]), (1, [(SIDE + k, 2 * k + 1) for k in range(4)])])
    give(1, [(3, [(LATE_0, 0), (LATE_0 + 1, 4), (LATE_2, 1), (LATE_2 + 1, 5)]),
             (0, [(B0 + k, k) for k in range(8)]), (2, [(SIDE + k, k) for k in range(8)])])
    for r, givers in enumerate(((1,), (0, 2), (1,), (0, 1, 2))):
        @pl.when(role == r)
        def _():
            for giver in givers:
                pltpu.make_async_remote_copy(
                    src_ref=staged.at[0], dst_ref=shares.at[giver], send_sem=share_send.at[0],
                    recv_sem=share_recv.at[giver], device_id=device_of_role(giver),
                    device_id_type=MESH).wait_recv()

    for i in range(16):
        value = line(i)
        for r in range(3):
            value = jnp.maximum(value, shares[r, i // 8, i % 8:i % 8 + 1, :])
        final[i] = jnp.broadcast_to(value, (8, 128))
    back[0] = final[0]
    for step in range(STEPS):
        for s, peer in peers(step, -1):
            pltpu.make_async_remote_copy(
                src_ref=final.at[s // 2], dst_ref=back.at[s], send_sem=back_send.at[0],
                recv_sem=back_recv.at[0], device_id=peer, device_id_type=MESH).start()
    pltpu.make_async_copy(back.at[pl.ds(1, 31)], back.at[pl.ds(1, 31)], back_recv.at[0]).wait()
    for i in range(16):
        final_line = jnp.where(low_half, back[2 * i], back[2 * i + 1])
        ord_in[i] = final_line

    def collect(j, _):
        at = pos_col[pl.ds(pl.multiple_of(j * 128, 128), 128), :]
        found = jnp.zeros((128, 128), jnp.float32)
        spot = lane[0:128, :]
        for i in range(16):
            found = jnp.where(at == spot + float(i * 128), ord_in[i][0:1, :], found)
        out[pl.ds(j, 1), :] = jnp.sum(found.T, axis=0, keepdims=True)
        return 0

    lax.fori_loop(0, 8, collect, 0)
    pltpu.make_async_copy(back.at[pl.ds(1, 31)], back.at[pl.ds(1, 31)], back_send.at[0]).wait()
    for r in range(4):
        @pl.when(role == r)
        def _():
            for index, (src, dst, to) in enumerate(sends[r]):
                for copy in share_rows(src, dst, to, index, dst - 8):
                    copy.wait_send()


def on_device(embeddings, cluster_ids, row_order):
    best = pl.pallas_call(
        kernel,
        out_shape=jax.ShapeDtypeStruct((8, 128), jnp.float32),
        in_specs=[pl.BlockSpec(memory_space=pltpu.VMEM)] * 3,
        out_specs=pl.BlockSpec(memory_space=pltpu.VMEM),
        scratch_shapes=[
            pltpu.VMEM((ROWS, D), jnp.bfloat16),
            pltpu.VMEM((CHUNK, ROWS), jnp.bfloat16),
            pltpu.VMEM((STEPS * CHUNK, D), jnp.bfloat16),
            pltpu.VMEM((CHUNKS * CHUNK, D), jnp.bfloat16),
            pltpu.VMEM((8, 128), jnp.float32),
            pltpu.VMEM((8, 128), jnp.float32),
            pltpu.VMEM((ROWS, 128), jnp.float32),
            pltpu.VMEM((ROWS, 128), jnp.float32),
            pltpu.VMEM((16, 8, 128), jnp.float32),
            pltpu.VMEM((32, 8, 128), jnp.float32),
            pltpu.VMEM((2 * CHUNKS, 8, 128), jnp.float32),
            pltpu.VMEM((CHUNKS * CHUNK, 128), jnp.float32),
            pltpu.VMEM((CHUNKS * CHUNK, 128), jnp.float32),
            pltpu.VMEM((2 * CHUNKS, 8, 128), jnp.float32),
            pltpu.VMEM((4, 2, 8, 128), jnp.float32),
            pltpu.VMEM((4, 2, 8, 128), jnp.float32),
            pltpu.VMEM((16, 8, 128), jnp.float32),
            pltpu.VMEM((32, 8, 128), jnp.float32),
            pltpu.SemaphoreType.DMA((STEPS,)),
            pltpu.SemaphoreType.DMA((STEPS,)),
            pltpu.SemaphoreType.DMA((STEPS,)),
            pltpu.SemaphoreType.DMA((STEPS,)),
            pltpu.SemaphoreType.DMA((16,)),
            pltpu.SemaphoreType.DMA((24,)),
            pltpu.SemaphoreType.DMA((16,)),
            pltpu.SemaphoreType.DMA((24,)),
            pltpu.SemaphoreType.DMA((4,)),
            pltpu.SemaphoreType.DMA((4,)),
            pltpu.SemaphoreType.DMA((1,)),
            pltpu.SemaphoreType.DMA((1,)),
        ],
        compiler_params=pltpu.CompilerParams(
            collective_id=0, has_side_effects=True, vmem_limit_bytes=56 * 1024 * 1024),
        name="best_match",
    )(embeddings, cluster_ids.reshape(8, 128), row_order.reshape(8, 128))
    return best.reshape(ROWS)


def solution(mesh):
    return jax.shard_map(
        on_device,
        mesh=mesh,
        in_specs=(P(("owner", "loop"), None), P(("owner", "loop")), P(("owner", "loop"))),
        out_specs=P(("owner", "loop")),
        check_vma=False,
    )
```

time: 277 us -> 110 us (0.40)
  Pallas kernels: 0 us -> 109 us
  blocking collectives: 84.1 us -> 0 us
  waiting for transfers between devices: 73.9 us -> 0 us
  matrix products: 50.4 us -> 0 us
  other arithmetic: 22.3 us -> 0 us
  local copies, waits for them, and re-layouts: 22.9 us -> 1.28 us
  between operations: 13.5 us -> 0.01 us
  starting transfers between devices: 9.56 us -> 0 us
    pallas_call x0 -> x1, Pallas kernels: none -> 109 us  [on_device(): pl.pallas_call(kernel, out_shape=jax.ShapeDtypeStruct((8, 128), jnp.float...]
    all_gather x1 -> x0, waiting for transfers between devices: 66.5 us -> none  [on_device(): keys = lax.all_gather(queries, 'loop', axis=0, tiled=True)]
    all_to_all x2 -> x0, blocking collectives: 63.1 us -> none  [the longest x1 48.7 us: on_device(): lax.all_to_all(outgoing.reshape(owners, capacity, payload.shape[1]), 'own...]
    dot_general x4 -> x0, matrix products: 50.4 us -> none  [one_block(): jnp.einsum('qd,kd->qk', block_rows, keys, preferred_element_type=jnp.floa...]
    all_gather x2 -> x0, blocking collectives: 21 us -> none  [the longest x1 10.7 us: on_device(): key_order = lax.all_gather(query_order, 'loop', axis=0, tiled=True)]
    gather x1 -> x0, local copies, waits for them, and re-layouts: 10.5 us -> none  [on_device(): return back.reshape(slots)[position]]
    all_to_all x2 -> x0, starting transfers between devices: 9.56 us -> none  [the longest x1 5.61 us: on_device(): lax.all_to_all(out_cluster.reshape(owners, capacity), 'owner', split_axis...]
    another operation x4 -> x0, other arithmetic: 9.15 us -> none
  transfers between devices with their start and end apart: 3 -> 0, of which waited for: 3 -> 0; matrix products, arithmetic and copies ran while one was open for 4% -> 0% of each run, Pallas kernels for 0% -> 0%
where the time goes in v1:
time: 110 us
  Pallas kernels  109 us (99%)
  local copies, waits for them, and re-layouts  1.28 us (1%)
    pallas_call x1, Pallas kernels, on_device(): pl.pallas_call(kernel, out_shape=jax.ShapeDtypeStruct((8, 128), jnp.float...  109 us

profile of v1, /device:TPU:1, one launch (start us, length us, event | category | flops | bytes accessed | tf_op | source)
XLA Modules:
  0.0 109.9 jit_solution(11763494293998806964)
XLA Ops:
  0.0 108.7 %best_match.1 = f32[8,128]{1,0:T(8,128)} custom-call(bf16[1024,768]{1,0:T(8,128)(2,1)} %emb.1, s32[8,128]{1,0:T(8,128)} %bitcast.4, s32[8,128]{1,0:T(8,128)} %bitcast.5), custom_call_target="tpu_custom_call" | custom-call | tf_op jit(solution)/shard_map/best_match/pallas_call | solution.py:407
  108.7 1.3 %copy.5 = f32[1024]{0:T(1024)} copy(f32[1024]{0:T(1024)} %bitcast.3) | data formatting | bytes 8192

commit v2 on v1

--- a/solution.py
+++ b/solution.py
@@ -17,6 +17,7 @@
 CHUNKS = 32
 FAR = float(2 ** 20)
 WINDOW = 3
+GROUP = 4
 
 OFFSETS = [
     [(0, 0), (2, 2)], [(1, 0), (3, 0)], [(0, 1), (0, 3)], [(1, 1), (3, 3)],
@@ -211,60 +212,50 @@
         at = n * CHUNK
         return pl.ds(at if isinstance(at, int) else pl.multiple_of(at, CHUNK), CHUNK)
 
-    def scores(m, n):
-        return lax.dot_general(rows[rows_of(m), :], rows[rows_of(n), :], (((1,), (1,)), ((), ())),
-                               preferred_element_type=jnp.float32)
-
-    def cross(m, n):
-        s = scores(m, n)
-        mine = ord_sub[rows_of(m), :]
-        best = row_best[rows_of(m), :]
-        for h in range(2):
-            part = s[:, h * 128:(h + 1) * 128]
-            mask = ord_lane[2 * n + h][0:1, :] < mine
-            best = jnp.maximum(best, jnp.where(mask, part, -1.0))
-            other = jnp.where(mask, -1.0, part).reshape(CHUNK // 8, 8, 128)
-            col_best[2 * n + h] = jnp.maximum(col_best[2 * n + h], jnp.max(other, axis=0))
-        row_best[rows_of(m), :] = best
-
-    def alone(n):
-        s = scores(n, n)
-        mine = ord_sub[rows_of(n), :]
-        best = row_best[rows_of(n), :]
-        for h in range(2):
-            mask = ord_lane[2 * n + h][0:1, :] < mine
-            best = jnp.maximum(best, jnp.where(mask, s[:, h * 128:(h + 1) * 128], -1.0))
-        row_best[rows_of(n), :] = best
+    def cross(ms, n):
+        held = jnp.concatenate([rows[rows_of(m), :] for m in ms], axis=0)
+        s = lax.dot_general(held, rows[rows_of(n), :], (((1,), (1,)), ((), ())), preferred_element_type=jnp.float32)
+        for k, m in enumerate(ms):
+            mine = ord_sub[rows_of(m), :]
+            best = row_best[rows_of(m), :]
+            for h in range(2):
+                part = s[k * CHUNK:(k + 1) * CHUNK, h * 128:(h + 1) * 128]
+                when = ord_lane[2 * n + h][0:1, :]
+                best = jnp.maximum(best, jnp.where(when < mine, part, -1.0))
+                other = jnp.where(mine < when, part, -1.0).reshape(CHUNK // 8, 8, 128)
+                col_best[2 * n + h] = jnp.maximum(col_best[2 * n + h], jnp.max(other, axis=0))
+            row_best[rows_of(m), :] = best
 
     tables = plan()
 
     def meet(s, name):
         events = [tables[r][s].get(name) for r in range(4)]
         n = by_role([e[0] if e else 0 for e in events])
-        depth = max(len(e[1]) for e in events if e)
+        lists = [[r for r in e[1] if r[1]] + ([(e[0], 1)] if e[2] else []) if e else [] for e in events]
+        depth = max(len(ranges) for ranges in lists)
+        if not depth:
+            return
         starts, counts = [], []
         for k in range(depth):
-            ranges = [e[1][k] if e and k < len(e[1]) else (0, 0) for e in events]
+            ranges = [ranges[k] if k < len(ranges) else (0, 0) for ranges in lists]
             starts.append(by_role([r[0] for r in ranges]))
             counts.append(by_role([r[1] for r in ranges]))
-        total = by_role([sum(r[1] for r in e[1]) if e else 0 for e in events])
-
-        def body(t, _):
+        total = by_role([sum(r[1] for r in ranges) for ranges in lists])
+
+        def member(t):
+            t = jnp.minimum(t, total - 1)
             m = t + starts[0]
             passed = counts[0]
             for k in range(1, depth):
                 m = jnp.where(t >= passed, t - passed + starts[k], m)
                 passed = passed + counts[k]
-            cross(m, n)
+            return m
+
+        def body(t, _):
+            cross([member(t * GROUP + k) for k in range(GROUP)], n)
             return 0
 
-        if any(sum(r[1] for r in e[1]) for e in events if e):
-            lax.fori_loop(0, total, body, 0)
-        selves = [1 if e and e[2] else 0 for e in events]
-        if any(selves):
-            @pl.when(by_role(selves) == 1)
-            def _():
-                alone(n)
+        lax.fori_loop(0, (total + GROUP - 1) // GROUP, body, 0)
 
     def share_rows(src, dst, to, send_index, recv_index):
         data = pltpu.make_async_remote_copy(

time: 110 us -> 89.7 us (0.82)
  Pallas kernels: 109 us -> 88.3 us
    pallas_call x1, Pallas kernels: 109 us -> 88.3 us  [on_device(): pl.pallas_call(kernel, out_shape=jax.ShapeDtypeStruct((8, 128), jnp.float...]
where the time goes in v2:
time: 89.7 us; the launch traced here: 89.6 us
  Pallas kernels  88.3 us (98%)
  local copies, waits for them, and re-layouts  1.28 us (1%)
    pallas_call x1, Pallas kernels, on_device(): pl.pallas_call(kernel, out_shape=jax.ShapeDtypeStruct((8, 128), jnp.float...  88.3 us

profile of v2, /device:TPU:1, one launch (start us, length us, event | category | flops | bytes accessed | tf_op | source)
XLA Modules:
  0.0 89.6 jit_solution(10267819043692925720)
XLA Ops:
  0.0 88.3 %best_match.1 = f32[8,128]{1,0:T(8,128)} custom-call(bf16[1024,768]{1,0:T(8,128)(2,1)} %emb.1, s32[8,128]{1,0:T(8,128)} %bitcast.4, s32[8,128]{1,0:T(8,128)} %bitcast.5), custom_call_target="tpu_custom_call" | custom-call | tf_op jit(solution)/shard_map/best_match/pallas_call | solution.py:398
  88.3 1.3 %copy.5 = f32[1024]{0:T(1024)} copy(f32[1024]{0:T(1024)} %bitcast.3) | data formatting | bytes 8192

commit v3 on v2

--- a/solution.py
+++ b/solution.py
@@ -17,12 +17,21 @@
 CHUNKS = 32
 FAR = float(2 ** 20)
 WINDOW = 3
-GROUP = 4
+WIDEST = 8
+
+
+def width(totals):
+    def cost(group):
+        return max(-(-total // group) for total in totals) * (2.3 + group)
+
+    return min(range(1, WIDEST + 1), key=cost)
+
 
 OFFSETS = [
     [(0, 0), (2, 2)], [(1, 0), (3, 0)], [(0, 1), (0, 3)], [(1, 1), (3, 3)],
     [(2, 1), (2, 3)], [(1, 3), (3, 1)], [(1, 2), (3, 2)], [(2, 0), (0, 2)],
 ]
+FAR_FIRST = (0, 4, 6, 3, 5, 7, 1, 2)
 
 
 def place(step):
@@ -30,6 +39,8 @@
 
 
 KEPT = ["q", "r", "p", "p", "q", "r", "p", "p"]
+RELAY_0 = [step for step in range(STEPS) if KEPT[step] == "q"]
+RELAY_2 = [step for step in range(STEPS) if KEPT[step] == "r"]
 TO_0 = [step for step in range(STEPS) if KEPT[step] in "pq"]
 TO_2 = [step for step in range(STEPS) if KEPT[step] in "pr"]
 SIDE, THIRD, LATE_2, B0, LATE_0 = 8, 12, 16, 20, 28
@@ -73,10 +84,10 @@
                 high += 1
                 events["C"] = (B0 + low, [(4, odd), (SIDE, high), (LATE_2, late_high)], False)
                 low += 1
-                if s in (2, 6):
+                if s - 2 in RELAY_0:
                     events["D"] = (LATE_0 + late_low, [(4, odd), (SIDE, high)], False)
                     late_low += 1
-                if s in (3, 7):
+                if s - 2 in RELAY_2:
                     events["D"] = (LATE_2 + late_high, [(0, even), (B0, low)], False)
                     late_high += 1
             steps.append(events)
@@ -157,23 +168,26 @@
 
     lax.fori_loop(0, ROWS // 128, normalize, 0)
 
-    def send(step, start):
-        for s, peer in peers(step, 1):
+    def send(half):
+        for s, peer in peers(half // 2, 1):
+            if s // 2 % 2 != half % 2:
+                continue
             data = pltpu.make_async_remote_copy(
                 src_ref=packed.at[pl.ds(s * CAP, CAP)], dst_ref=rows.at[pl.ds(s * CAP, CAP)],
-                send_sem=send_sem.at[step], recv_sem=recv_sem.at[step], device_id=peer, device_id_type=MESH)
+                send_sem=send_sem.at[half], recv_sem=recv_sem.at[half], device_id=peer, device_id_type=MESH)
             data.start()
             when = pltpu.make_async_remote_copy(
                 src_ref=ord_out.at[s // 2], dst_ref=ord_in.at[s],
-                send_sem=osend_sem.at[step], recv_sem=orecv_sem.at[step], device_id=peer, device_id_type=MESH)
+                send_sem=osend_sem.at[half], recv_sem=orecv_sem.at[half], device_id=peer, device_id_type=MESH)
             when.start()
 
-    def exchange_wait(step, sem, osem):
-        skip = 1 if step == 0 else 0
-        r = pl.ds(place(step) * CHUNK + skip * CAP, CHUNK - skip * CAP)
-        pltpu.make_async_copy(packed.at[r], rows.at[r], sem.at[step]).wait()
-        o = pl.ds(4 * place(step) + skip, 4 - skip)
-        pltpu.make_async_copy(ord_in.at[o], ord_in.at[o], osem.at[step]).wait()
+    def exchange_wait(half, sem, osem):
+        skip = 1 if half == 0 else 0
+        first = 4 * place(half // 2) + 2 * (half % 2) + skip
+        r = pl.ds(first * CAP, (2 - skip) * CAP)
+        pltpu.make_async_copy(packed.at[r], rows.at[r], sem.at[half]).wait()
+        o = pl.ds(first, 2 - skip)
+        pltpu.make_async_copy(ord_in.at[o], ord_in.at[o], osem.at[half]).wait()
 
     lane = lax.broadcasted_iota(jnp.int32, (1024, 128), 1).astype(jnp.float32)
     for step in range(STEPS):
@@ -192,8 +206,9 @@
             rows[0:CAP, :] = block[0:CAP, :]
             ord_in[0] = ord_out[0]
             pl.semaphore_wait(barrier, 34)
-        if step < WINDOW:
-            send(step, True)
+        for half in (2 * step, 2 * step + 1):
+            if half < WINDOW:
+                send(half)
 
     def clear(i, _):
         row_best[pl.ds(pl.multiple_of(i * CHUNK, CHUNK), CHUNK), :] = jnp.full((CHUNK, 128), -1.0, jnp.float32)
@@ -240,7 +255,8 @@
             ranges = [ranges[k] if k < len(ranges) else (0, 0) for ranges in lists]
             starts.append(by_role([r[0] for r in ranges]))
             counts.append(by_role([r[1] for r in ranges]))
-        total = by_role([sum(r[1] for r in ranges) for ranges in lists])
+        totals = [sum(r[1] for r in ranges) for ranges in lists]
+        total, group = by_role(totals), width(totals)
 
         def member(t):
             t = jnp.minimum(t, total - 1)
@@ -252,31 +268,45 @@
             return m
 
         def body(t, _):
-            cross([member(t * GROUP + k) for k in range(GROUP)], n)
+            cross([member(t * group + k) for k in range(group)], n)
             return 0
 
-        lax.fori_loop(0, (total + GROUP - 1) // GROUP, body, 0)
-
-    def share_rows(src, dst, to, send_index, recv_index):
+        lax.fori_loop(0, (total + group - 1) // group, body, 0)
+
+    def share_rows(src, dst, h, to, send_index):
+        recv_index = 2 * (dst - 8) + h
         data = pltpu.make_async_remote_copy(
-            src_ref=rows.at[rows_of(src)], dst_ref=rows.at[rows_of(dst)],
+            src_ref=rows.at[pl.ds(src * CHUNK + h * 128, 128)], dst_ref=rows.at[pl.ds(dst * CHUNK + h * 128, 128)],
             send_sem=ysend_sem.at[send_index], recv_sem=yrecv_sem.at[recv_index],
             device_id=device_of_role(to), device_id_type=MESH)
         when = pltpu.make_async_remote_copy(
-            src_ref=ord_lane.at[pl.ds(2 * src, 2)], dst_ref=ord_lane.at[pl.ds(2 * dst, 2)],
+            src_ref=ord_lane.at[2 * src + h], dst_ref=ord_lane.at[2 * dst + h],
             send_sem=yosend_sem.at[send_index], recv_sem=yorecv_sem.at[recv_index],
             device_id=device_of_role(to), device_id_type=MESH)
         return data, when
 
     sends = [[], [], [], []]
 
-    def forward(r, src, dst, to):
-        @pl.when(role == r)
-        def _():
-            index = len(sends[r])
-            for copy in share_rows(src, dst, to, index, dst - 8):
-                copy.start()
-            sends[r].append((src, dst, to))
+    def pass_on(r, src, dst, h, to):
+        for copy in share_rows(src, dst, h, to, len(sends[r])):
+            copy.start()
+        sends[r].append((src, dst, h, to))
+
+    def forward(s, h):
+        n = place(s)
+        for r in range(4):
+            @pl.when(role == r)
+            def _():
+                if r == 0:
+                    pass_on(0, n, B0 + s, h, 1)
+                if r == 1:
+                    pass_on(1, n, SIDE + s // 2, h, 0 if s % 2 == 0 else 2)
+                if r == 2:
+                    pass_on(2, n, SIDE + s, h, 1)
+                if r == 3 and KEPT[s] in "pq":
+                    pass_on(3, n, THIRD + TO_0.index(s), h, 0)
+                if r == 3 and KEPT[s] in "pr":
+                    pass_on(3, n, THIRD + TO_2.index(s), h, 2)
 
     def arrive(s, name):
         events = [tables[r][s].get(name) for r in range(4)]
@@ -287,34 +317,27 @@
             @pl.when(role == r)
             def _():
                 n = events[r][0]
-                for copy in share_rows(n, n, (r + 1) % 4, 0, n - 8):
-                    copy.wait_recv()
-                if r in (0, 2) and name == "C" and n in (THIRD, THIRD + 3):
-                    index = len(sends[r])
-                    late = LATE_0 if r == 0 else LATE_2
-                    late = late + (n - THIRD) // 3
-                    for copy in share_rows(n, late, 1, index, late - 8):
-                        copy.start()
-                    sends[r].append((n, late, 1))
+                relays = {0: RELAY_0, 2: RELAY_2}.get(r, [])
+                for h in range(2):
+                    for copy in share_rows(n, n, h, (r + 1) % 4, 0):
+                        copy.wait_recv()
+                    if name == "C" and s - 1 in relays:
+                        late = (LATE_0 if r == 0 else LATE_2) + relays.index(s - 1)
+                        pass_on(r, n, late, h, 1)
                 spread(n)
 
     low_half = lax.broadcasted_iota(jnp.int32, (8, 128), 1) < CAP
     for s in range(STEPS + 1):
         if s < STEPS:
             n = place(s)
-            exchange_wait(s, send_sem, osend_sem)
-            if s + WINDOW < STEPS:
-                send(s + WINDOW, True)
-            exchange_wait(s, recv_sem, orecv_sem)
             for h in range(2):
+                half = 2 * s + h
+                exchange_wait(half, send_sem, osend_sem)
+                if half + WINDOW < 2 * STEPS:
+                    send(half + WINDOW)
+                exchange_wait(half, recv_sem, orecv_sem)
                 ord_lane[2 * n + h] = jnp.where(low_half, ord_in[4 * n + 2 * h], ord_in[4 * n + 2 * h + 1])
-            forward(0, n, B0 + s, 1)
-            forward(2, n, SIDE + s, 1)
-            forward(1, n, SIDE + s // 2, 0 if s % 2 == 0 else 2)
-            if KEPT[s] in "pq":
-                forward(3, n, THIRD + TO_0.index(s), 0)
-            if KEPT[s] in "pr":
-                forward(3, n, THIRD + TO_2.index(s), 2)
+                forward(s, h)
             spread(n)
             meet(s, "A")
         for names in ("BC", "D"):
@@ -343,13 +366,14 @@
                     src_ref=staged.at[to], dst_ref=shares.at[r], send_sem=share_send.at[to],
                     recv_sem=share_recv.at[r], device_id=device_of_role(to), device_id_type=MESH))
                 copies[-1].start()
-            for copy in copies:
-                copy.wait_send()
 
     give(0, [(3, [(THIRD + k, t) for k, t in enumerate(TO_0)]), (1, [(SIDE + k, 2 * k) for k in range(4)])])
     give(2, [(3, [(THIRD + k, t) for k, t in enumerate(TO_2)]), (1, [(SIDE + k, 2 * k + 1) for k in range(4)])])
-    give(1, [(3, [(LATE_0, 0), (LATE_0 + 1, 4), (LATE_2, 1), (LATE_2 + 1, 5)]),
+    late = [(LATE_0 + k, t) for k, t in enumerate(RELAY_0)] + [(LATE_2 + k, t) for k, t in enumerate(RELAY_2)]
+    give(1, [(3, late),
              (0, [(B0 + k, k) for k in range(8)]), (2, [(SIDE + k, k) for k in range(8)])])
+    for i in range(16):
+        final[i] = jnp.broadcast_to(line(i), (8, 128))
     for r, givers in enumerate(((1,), (0, 2), (1,), (0, 1, 2))):
         @pl.when(role == r)
         def _():
@@ -360,12 +384,12 @@
                     device_id_type=MESH).wait_recv()
 
     for i in range(16):
-        value = line(i)
-        for r in range(3):
+        value = shares[0, i // 8, i % 8:i % 8 + 1, :]
+        for r in range(1, 3):
             value = jnp.maximum(value, shares[r, i // 8, i % 8:i % 8 + 1, :])
-        final[i] = jnp.broadcast_to(value, (8, 128))
+        final[i] = jnp.maximum(final[i], value)
     back[0] = final[0]
-    for step in range(STEPS):
+    for step in FAR_FIRST:
         for s, peer in peers(step, -1):
             pltpu.make_async_remote_copy(
                 src_ref=final.at[s // 2], dst_ref=back.at[s], send_sem=back_send.at[0],
@@ -385,12 +409,19 @@
         return 0
 
     lax.fori_loop(0, 8, collect, 0)
+    for r, owners in enumerate(((3, 1), (3, 0, 2), (3, 1))):
+        @pl.when(role == r)
+        def _():
+            for to in owners:
+                pltpu.make_async_remote_copy(
+                    src_ref=staged.at[to], dst_ref=shares.at[r], send_sem=share_send.at[to],
+                    recv_sem=share_recv.at[r], device_id=device_of_role(to), device_id_type=MESH).wait_send()
     pltpu.make_async_copy(back.at[pl.ds(1, 31)], back.at[pl.ds(1, 31)], back_send.at[0]).wait()
     for r in range(4):
         @pl.when(role == r)
         def _():
-            for index, (src, dst, to) in enumerate(sends[r]):
-                for copy in share_rows(src, dst, to, index, dst - 8):
+            for index, (src, dst, h, to) in enumerate(sends[r]):
+                for copy in share_rows(src, dst, h, to, index):
                     copy.wait_send()
 
 
@@ -419,14 +450,14 @@
             pltpu.VMEM((4, 2, 8, 128), jnp.float32),
             pltpu.VMEM((16, 8, 128), jnp.float32),
             pltpu.VMEM((32, 8, 128), jnp.float32),
-            pltpu.SemaphoreType.DMA((STEPS,)),
-            pltpu.SemaphoreType.DMA((STEPS,)),
-            pltpu.SemaphoreType.DMA((STEPS,)),
-            pltpu.SemaphoreType.DMA((STEPS,)),
-            pltpu.SemaphoreType.DMA((16,)),
-            pltpu.SemaphoreType.DMA((24,)),
-            pltpu.SemaphoreType.DMA((16,)),
-            pltpu.SemaphoreType.DMA((24,)),
+            pltpu.SemaphoreType.DMA((2 * STEPS,)),
+            pltpu.SemaphoreType.DMA((2 * STEPS,)),
+            pltpu.SemaphoreType.DMA((2 * STEPS,)),
+            pltpu.SemaphoreType.DMA((2 * STEPS,)),
+            pltpu.SemaphoreType.DMA((32,)),
+            pltpu.SemaphoreType.DMA((48,)),
+            pltpu.SemaphoreType.DMA((32,)),
+            pltpu.SemaphoreType.DMA((48,)),
             pltpu.SemaphoreType.DMA((4,)),
             pltpu.SemaphoreType.DMA((4,)),
             pltpu.SemaphoreType.DMA((1,)),

time: 89.7 us -> 88.7 us (0.989)
  Pallas kernels: 88.3 us -> 87.2 us
    pallas_call x1, Pallas kernels: 88.3 us -> 87.2 us  [on_device(): pl.pallas_call(kernel, out_shape=jax.ShapeDtypeStruct((8, 128), jnp.float...]
where the time goes in v3:
time: 88.7 us; the launch traced here: 88.5 us
  Pallas kernels  87.2 us (98%)
  local copies, waits for them, and re-layouts  1.28 us (1%)
    pallas_call x1, Pallas kernels, on_device(): pl.pallas_call(kernel, out_shape=jax.ShapeDtypeStruct((8, 128), jnp.float...  87.2 us

profile of v3, /device:TPU:1, one launch (start us, length us, event | category | flops | bytes accessed | tf_op | source)
XLA Modules:
  0.0 88.5 jit_solution(18313309761364142300)
XLA Ops:
  0.0 87.2 %best_match.1 = f32[8,128]{1,0:T(8,128)} custom-call(bf16[1024,768]{1,0:T(8,128)(2,1)} %emb.1, s32[8,128]{1,0:T(8,128)} %bitcast.4, s32[8,128]{1,0:T(8,128)} %bitcast.5), custom_call_target="tpu_custom_call" | custom-call | tf_op jit(solution)/shard_map/best_match/pallas_call | solution.py:429
  87.2 1.3 %copy.5 = f32[1024]{0:T(1024)} copy(f32[1024]{0:T(1024)} %bitcast.3) | data formatting | bytes 8192

commit v4 on v3

--- a/solution.py
+++ b/solution.py
@@ -16,6 +16,7 @@
 STEPS = 8
 CHUNKS = 32
 FAR = float(2 ** 20)
+AHEAD = 3
 WINDOW = 3
 WIDEST = 8
 
@@ -190,7 +191,8 @@
         pltpu.make_async_copy(ord_in.at[o], ord_in.at[o], osem.at[half]).wait()
 
     lane = lax.broadcasted_iota(jnp.int32, (1024, 128), 1).astype(jnp.float32)
-    for step in range(STEPS):
+
+    def pack(step):
         first = place(step) * CHUNK
         wanted = lax.broadcasted_iota(jnp.int32, (CHUNK, 128), 0).astype(jnp.float32) + float(first)
         for j in range(8):
@@ -205,6 +207,10 @@
         if step == 0:
             rows[0:CAP, :] = block[0:CAP, :]
             ord_in[0] = ord_out[0]
+
+    for step in range(AHEAD):
+        pack(step)
+        if step == 0:
             pl.semaphore_wait(barrier, 34)
         for half in (2 * step, 2 * step + 1):
             if half < WINDOW:
@@ -338,6 +344,8 @@
                 exchange_wait(half, recv_sem, orecv_sem)
                 ord_lane[2 * n + h] = jnp.where(low_half, ord_in[4 * n + 2 * h], ord_in[4 * n + 2 * h + 1])
                 forward(s, h)
+            if s + AHEAD < STEPS:
+                pack(s + AHEAD)
             spread(n)
             meet(s, "A")
         for names in ("BC", "D"):

time: 88.7 us -> 88.3 us (level)
  no operation moved by 1% of the time
where the time goes in v4:
time: 88.3 us; the launch traced here: 88.1 us
  Pallas kernels  86.8 us (98%)
  local copies, waits for them, and re-layouts  1.28 us (1%)
    pallas_call x1, Pallas kernels, on_device(): pl.pallas_call(kernel, out_shape=jax.ShapeDtypeStruct((8, 128), jnp.float...  86.8 us

profile of v4, /device:TPU:1, one launch (start us, length us, event | category | flops | bytes accessed | tf_op | source)
XLA Modules:
  0.0 88.1 jit_solution(18361342670731275851)
XLA Ops:
  0.0 86.8 %best_match.1 = f32[8,128]{1,0:T(8,128)} custom-call(bf16[1024,768]{1,0:T(8,128)(2,1)} %emb.1, s32[8,128]{1,0:T(8,128)} %bitcast.4, s32[8,128]{1,0:T(8,128)} %bitcast.5), custom_call_target="tpu_custom_call" | custom-call | tf_op jit(solution)/shard_map/best_match/pallas_call | solution.py:437
  86.8 1.3 %copy.5 = f32[1024]{0:T(1024)} copy(f32[1024]{0:T(1024)} %bitcast.3) | data formatting | bytes 8192
